TPU v7x, 128 devices: a whole 4x4x4 slice. The times are simulated.
128 devices in a mesh: dp: 16 (over x, z_hi, core), tensor: 8 (over z_lo, y).
Axes of the slice: x: 4, y: 4, z: 4 (z_hi: 2, z_lo: 2; z = z_hi * 2 + z_lo), core: 2. Of those that a mesh axis runs over, the one named last changes fastest.
Arguments:
- tokens: bfloat16 [16, 1024, 2048], P('dp', 'tensor'), may hold values from -6 to 6
- query_weight: bfloat16 [2048, 2048], P(None, 'tensor'), may hold values from -0.125 to 0.125
- key_weight: bfloat16 [2048, 2048], P(None, 'tensor'), may hold values from -0.125 to 0.125
- value_weight: bfloat16 [2048, 2048], P(None, 'tensor'), may hold values from -0.125 to 0.125
- output_weight: bfloat16 [2048, 2048], P('tensor'), may hold values from -2 to 2
- gate_weight: bfloat16 [2048, 5504], P(None, 'tensor'), may hold values from -0.125 to 0.125
- up_weight: bfloat16 [2048, 5504], P(None, 'tensor'), may hold values from -0.125 to 0.125
- down_weight: bfloat16 [5504, 2048], P('tensor'), may hold values from -0.109375 to 0.109375
- attn_gain: float32 [2048], replicated, may hold values from 0.1 to 1.9
- mlp_gain: float32 [2048], replicated, may hold values from 0.1 to 1.9
- cotangent: bfloat16 [16, 1024, 2048], P('dp', 'tensor'), may hold values from -6 to 6
Outputs:
- activations: bfloat16 [16, 1024, 2048], P('dp', 'tensor')
- input_grad: float32 [16, 1024, 2048], P('dp', 'tensor')
- query_weight_gradient: float32 [2048, 2048], P(None, 'tensor')
- key_weight_gradient: float32 [2048, 2048], P(None, 'tensor')
- value_weight_gradient: float32 [2048, 2048], P(None, 'tensor')
- output_weight_gradient: float32 [2048, 2048], P('tensor')
- gate_weight_gradient: float32 [2048, 5504], P(None, 'tensor')
- up_weight_gradient: float32 [2048, 5504], P(None, 'tensor')
- down_weight_gradient: float32 [5504, 2048], P('tensor')
- attn_gain_grad: float32 [2048], P('tensor')
- mlp_gain_grad: float32 [2048], P('tensor')
All inputs are finite; a program needn't handle non-finite values.
Results may differ from a plain program's by a relative error of at most 0.03.
Values may be sent and summed in bfloat16 or wider, within the bound.
A program may use at most 192 MiB of HBM per device.

v0:
```python
import jax
import jax.numpy as jnp
from jax import lax
from jax.sharding import PartitionSpec as P

HEAD_DIM = 128


norm_eps = 1e-05
rope_base = 10000.0
block_limit = 512


def in_blocks(x, dim, length):
    before, after = (x.shape[:dim], x.shape[dim + 1 :])
    return jnp.moveaxis(x.reshape(*before, length, -1, *after), dim, 0)


def summed_on_arrival(x, axis, dim):
    blocks = in_blocks(x, dim, lax.axis_size(axis))
    arrived = lax.all_to_all(blocks, axis, split_axis=0, concat_axis=0, tiled=True)
    return arrived.sum(axis=0)


def packed_total(arrays, axis):
    ends = [0]
    for a in arrays:
        ends.append(ends[-1] + a.size)
    subtotal = lax.psum(jnp.concatenate([a.ravel() for a in arrays]), axis)
    return tuple((subtotal[b:e].reshape(a.shape) for a, b, e in zip(arrays, ends, ends[1:])))


def tables(length, head_dim):
    half = head_dim // 2
    freqs = rope_base ** (-(2.0 * jnp.arange(half, dtype=jnp.float32)) / head_dim)
    angles = jnp.arange(length, dtype=jnp.float32)[:, None] * freqs[None, :]
    cosine_table = jnp.cos(angles)
    sine_table = jnp.sin(angles)
    return (
        jnp.concatenate([cosine_table, cosine_table], 1),
        jnp.concatenate([sine_table, sine_table], 1),
    )


def apply_rotation(values, cosine_table, sine_table):
    half = values.shape[-1] // 2
    turned = jnp.concatenate([-values[..., half:], values[..., :half]], -1)
    return values * cosine_table[:, None, :] + turned * sine_table[:, None, :]


def unrotate(grads, cosine_table, sine_table):
    half = grads.shape[-1] // 2
    moved = grads * sine_table[:, None, :]
    turned = jnp.concatenate([moved[..., half:], -moved[..., :half]], -1)
    return grads * cosine_table[:, None, :] + turned


def normalize(values):
    factor = lax.rsqrt(jnp.mean(values * values, axis=-1, keepdims=True) + norm_eps)
    return (values * factor, factor)


def norm_back(grads, unit, factor):
    return factor * (grads - unit * jnp.mean(grads * unit, axis=-1, keepdims=True))


def apply_projection(form, left, right):
    return jnp.einsum(form, left, right, preferred_element_type=jnp.float32)


def causal(start, rows, stop):
    places = start + jnp.arange(rows, dtype=jnp.int32)[:, None]
    return (jnp.arange(stop, dtype=jnp.int32)[None, :] <= places)[None, None, :, :]


def per_device(
    tokens,
    query_weight,
    key_weight,
    value_weight,
    output_weight,
    gate_weight,
    up_weight,
    down_weight,
    attn_gain,
    mlp_gain,
    cotangent,
):
    sequences, local_len, width = tokens.shape
    length = local_len * lax.axis_size("tensor")
    head_dim = HEAD_DIM
    local_heads = query_weight.shape[1] // head_dim
    rows = min(block_limit, length)
    blocks = length // rows
    scale = head_dim ** (-0.5)
    cosine_table, sine_table = tables(length, head_dim)
    head_layout = (sequences, length, local_heads, head_dim)
    inputs = tokens.astype(jnp.float32)
    unit_one, factor_one = normalize(inputs)
    normalized_first = (unit_one * attn_gain).astype(jnp.bfloat16)
    collected_first = lax.all_gather(normalized_first, "tensor", axis=1, tiled=True)
    query_rows = apply_rotation(
        apply_projection("ozb,bv->ozv", collected_first, query_weight).reshape(head_layout),
        cosine_table,
        sine_table,
    ).astype(jnp.bfloat16)
    key = apply_rotation(
        apply_projection("ozb,bv->ozv", collected_first, key_weight).reshape(head_layout),
        cosine_table,
        sine_table,
    ).astype(jnp.bfloat16)
    value_rows = (
        apply_projection("ozb,bv->ozv", collected_first, value_weight)
        .astype(jnp.bfloat16)
        .reshape(head_layout)
    )
    outputs = []
    log_totals = []
    for block in range(blocks):
        start = block * rows
        stop = start + rows
        scores = (
            apply_projection("sqhd,skhd->shqk", query_rows[:, start:stop], key[:, :stop]) * scale
        )
        scores = jnp.where(causal(start, rows, stop), scores, -1e30)
        highest_score = jnp.max(scores, -1, keepdims=True)
        raised = jnp.exp(scores - highest_score)
        totals = jnp.sum(raised, -1, keepdims=True)
        probs_low = (raised / totals).astype(jnp.bfloat16)
        outputs.append(apply_projection("shqk,skhd->sqhd", probs_low, value_rows[:, :stop]))
        log_totals.append(highest_score + jnp.log(totals))
    head_outputs = (
        jnp.concatenate(outputs, 1)
        .astype(jnp.bfloat16)
        .reshape(sequences, length, local_heads * head_dim)
    )
    attention_parts = apply_projection("ahw,wz->ahz", head_outputs, output_weight)
    attn_branch = lax.psum_scatter(
        attention_parts.astype(jnp.bfloat16), "tensor", scatter_dimension=1, tiled=True
    ).astype(jnp.float32)
    residual_stream = inputs + attn_branch
    unit_two, factor_two = normalize(residual_stream)
    normalized_second = (unit_two * mlp_gain).astype(jnp.bfloat16)
    collected_second = lax.all_gather(normalized_second, "tensor", axis=1, tiled=True)
    gate_activation = apply_projection("jpq,qa->jpa", collected_second, gate_weight)
    up_activation = apply_projection("jpq,qa->jpa", collected_second, up_weight)
    sigma = jax.nn.sigmoid(gate_activation)
    swish = gate_activation * sigma
    hidden_activation = (swish * up_activation).astype(jnp.bfloat16)
    feedforward_parts = apply_projection("rum,mj->ruj", hidden_activation, down_weight)
    mlp_branch = lax.psum_scatter(
        feedforward_parts.astype(jnp.bfloat16), "tensor", scatter_dimension=1, tiled=True
    ).astype(jnp.float32)
    activations = (residual_stream + mlp_branch).astype(jnp.bfloat16)
    grad_out = cotangent.astype(jnp.float32)
    feedforward_gradient_total = lax.all_gather(cotangent, "tensor", axis=1, tiled=True)
    down_weight_gradient = apply_projection(
        "kox,koj->xj", hidden_activation, feedforward_gradient_total
    )
    hidden_gradient = apply_projection("cyi,bi->cyb", feedforward_gradient_total, down_weight)
    gate_gradient = (
        hidden_gradient * up_activation * sigma * (1.0 + gate_activation * (1.0 - sigma))
    ).astype(jnp.bfloat16)
    up_gradient = (hidden_gradient * swish).astype(jnp.bfloat16)
    gate_weight_gradient = apply_projection("zoy,zok->yk", collected_second, gate_gradient)
    up_weight_gradient = apply_projection("zoy,zok->yk", collected_second, up_gradient)
    feedforward_backward_parts = apply_projection(
        "ngp,tp->ngt", gate_gradient, gate_weight
    ) + apply_projection("ngp,tp->ngt", up_gradient, up_weight)
    grad_normed_two = lax.psum_scatter(
        feedforward_backward_parts.astype(jnp.bfloat16), "tensor", scatter_dimension=1, tiled=True
    ).astype(jnp.float32)
    gain_two = jnp.sum(grad_normed_two * unit_two, axis=(0, 1))
    grad_resid = grad_out + norm_back(grad_normed_two * mlp_gain, unit_two, factor_two)
    down_weight_gradient, gate_weight_gradient, up_weight_gradient = (
        lax.psum(down_weight_gradient.astype(jnp.bfloat16), "dp").astype(jnp.float32),
        lax.psum(gate_weight_gradient.astype(jnp.bfloat16), "dp").astype(jnp.float32),
        lax.psum(up_weight_gradient.astype(jnp.bfloat16), "dp").astype(jnp.float32),
    )
    attention_gradient_total = lax.all_gather(
        grad_resid.astype(jnp.bfloat16), "tensor", axis=1, tiled=True
    )
    output_weight_gradient = apply_projection("xkb,xkf->bf", head_outputs, attention_gradient_total)
    grad_heads = (
        apply_projection("tzg,kg->tzk", attention_gradient_total, output_weight)
        .astype(jnp.bfloat16)
        .reshape(head_layout)
    )
    query_parts = []
    grad_key = jnp.zeros(head_layout, jnp.float32)
    grad_value = jnp.zeros(head_layout, jnp.float32)
    for block in range(blocks):
        start = block * rows
        stop = start + rows
        q_block = query_rows[:, start:stop]
        scores = apply_projection("sqhd,skhd->shqk", q_block, key[:, :stop]) * scale
        scores = jnp.where(causal(start, rows, stop), scores, -1e30)
        probs = jnp.exp(scores - log_totals[block])
        probs_low = probs.astype(jnp.bfloat16)
        grad_block = grad_heads[:, start:stop]
        grad_value = grad_value.at[:, :stop].add(
            apply_projection("shqk,sqhd->skhd", probs_low, grad_block)
        )
        grad_probs = apply_projection("sqhd,skhd->shqk", grad_block, value_rows[:, :stop])
        inner = jnp.sum(probs * grad_probs, -1, keepdims=True)
        grad_scores = (probs * (grad_probs - inner) * scale).astype(jnp.bfloat16)
        query_parts.append(apply_projection("shqk,skhd->sqhd", grad_scores, key[:, :stop]))
        grad_key = grad_key.at[:, :stop].add(
            apply_projection("shqk,sqhd->skhd", grad_scores, q_block)
        )
    flat_shape = (sequences, length, local_heads * head_dim)
    query_gradient = (
        unrotate(jnp.concatenate(query_parts, 1), cosine_table, sine_table)
        .astype(jnp.bfloat16)
        .reshape(flat_shape)
    )
    key_gradient_reduced = (
        unrotate(grad_key, cosine_table, sine_table).astype(jnp.bfloat16).reshape(flat_shape)
    )
    value_gradient_reduced = grad_value.astype(jnp.bfloat16).reshape(flat_shape)
    query_weight_gradient = apply_projection("kwh,kwj->hj", collected_first, query_gradient)
    key_weight_gradient = apply_projection("kwh,kwj->hj", collected_first, key_gradient_reduced)
    value_weight_gradient = apply_projection("kwh,kwj->hj", collected_first, value_gradient_reduced)
    attn_back_terms = (
        apply_projection("ugv,yv->ugy", query_gradient, query_weight)
        + apply_projection("ugv,yv->ugy", key_gradient_reduced, key_weight)
        + apply_projection("ugv,yv->ugy", value_gradient_reduced, value_weight)
    )
    grad_normed_one = lax.psum_scatter(
        attn_back_terms.astype(jnp.bfloat16), "tensor", scatter_dimension=1, tiled=True
    ).astype(jnp.float32)
    gain_one = jnp.sum(grad_normed_one * unit_one, axis=(0, 1))
    input_grad = grad_resid + norm_back(grad_normed_one * attn_gain, unit_one, factor_one)
    gain_grads = summed_on_arrival(jnp.stack([gain_one, gain_two]), "tensor", 1)
    (
        query_weight_gradient,
        key_weight_gradient,
        value_weight_gradient,
        output_weight_gradient,
        gain_grads,
    ) = tuple(
        (
            part.astype(jnp.float32)
            for part in packed_total(
                (
                    query_weight_gradient.astype(jnp.bfloat16),
                    key_weight_gradient.astype(jnp.bfloat16),
                    value_weight_gradient.astype(jnp.bfloat16),
                    output_weight_gradient.astype(jnp.bfloat16),
                    gain_grads.astype(jnp.bfloat16),
                ),
                "dp",
            )
        )
    )
    return (
        activations,
        input_grad,
        query_weight_gradient,
        key_weight_gradient,
        value_weight_gradient,
        output_weight_gradient,
        gate_weight_gradient,
        up_weight_gradient,
        down_weight_gradient,
        gain_grads[0],
        gain_grads[1],
    )


def solution(mesh):
    placed = (
        P("dp", "tensor", None),
        P(None, "tensor"),
        P(None, "tensor"),
        P(None, "tensor"),
        P("tensor", None),
        P(None, "tensor"),
        P(None, "tensor"),
        P("tensor", None),
        P(),
        P(),
        P("dp", "tensor", None),
    )
    return jax.shard_map(
        per_device,
        mesh=mesh,
        in_specs=placed,
        out_specs=(
            P("dp", "tensor", None),
            P("dp", "tensor", None),
            P(None, "tensor"),
            P(None, "tensor"),
            P(None, "tensor"),
            P("tensor", None),
            P(None, "tensor"),
            P(None, "tensor"),
            P("tensor", None),
            P("tensor"),
            P("tensor"),
        ),
        check_vma=False,
    )
```

profile of v0, /device:TPU:1, one launch (start us, length us, event | category | flops | bytes accessed | tf_op | source)
XLA Modules:
  0.0 901.2 jit_solution(16659691458032632627)
XLA Ops:
  17.2 49.5 %all-gather.5.cloned.1.call-done = bf16[1,1024,2048]{2,1,0:T(8,128)(2,1)} async-done(((bf16[1,128,2048]{2,1,0:T(8,128)(2,1)}), bf16[1,1024,2048]{2,1,0:T(8,128)(2,1)}) %all-gather.5.cloned.1.call-update) | async-done | bytes 4194320 | tf_op jit(solution)/shard_map/all_gather | solution.py:101
  66.7 3.8 fusion.25
  74.7 2.5 copy.85
  77.3 4.8 fusion.27
  82.0 2.5 copy.78
  84.5 2.4 copy.129
  86.9 2.4 copy.130
  103.6 3.3 convert_bitcast_fusion.1
  107.0 52.0 %reduce-scatter.5.cloned.1.call-done = bf16[1,128,2048]{2,1,0:T(8,128)(2,1)} async-done(((bf16[1,1024,2048]{2,1,0:T(8,128)(2,1)}), bf16[1,128,2048]{2,1,0:T(8,128)(2,1)}) %reduce-scatter.5.cloned.1.call-update) | async-done | bytes 524304 | tf_op jit(solution)/shard_map/reduce_scatter | solution.py:138
  163.0 50.9 %all-gather.7.cloned.1.call-done = bf16[1,1024,2048]{2,1,0:T(8,128)(2,1)} async-done(((bf16[1,128,2048]{2,1,0:T(8,128)(2,1)}), bf16[1,1024,2048]{2,1,0:T(8,128)(2,1)}) %all-gather.7.cloned.1.call-update) | async-done | bytes 4194320 | tf_op jit(solution)/shard_map/all_gather | solution.py:144
  213.9 7.9 fusion.15
  221.8 4.7 fusion.17
  226.5 40.4 %all-gather.9.cloned.1.call-done = bf16[1,1024,2048]{2,1,0:T(8,128)(2,1)} async-done(((bf16[1,128,2048]{2,1,0:T(8,128)(2,1)}), bf16[1,1024,2048]{2,1,0:T(8,128)(2,1)}) %all-gather.9.cloned.1.call-update) | async-done | bytes 4194320 | tf_op jit(solution)/shard_map/all_gather | solution.py:156
  266.8 8.2 multiply_convert_fusion.1
  275.1 3.5 fusion.191
  278.6 5.3 fusion.2
  284.0 52.0 %reduce-scatter.9.cloned.1.call-done = bf16[1,128,2048]{2,1,0:T(8,128)(2,1)} async-done(((bf16[1,1024,2048]{2,1,0:T(8,128)(2,1)}), bf16[1,128,2048]{2,1,0:T(8,128)(2,1)}) %reduce-scatter.9.cloned.1.call-update) | async-done | bytes 524304 | tf_op jit(solution)/shard_map/reduce_scatter | solution.py:170
  337.7 2.6 fusion.181
  342.6 49.2 %all-gather.11.cloned.1.call-done = bf16[1,1024,2048]{2,1,0:T(8,128)(2,1)} async-done(((bf16[1,128,2048]{2,1,0:T(8,128)(2,1)}), bf16[1,1024,2048]{2,1,0:T(8,128)(2,1)}) %all-gather.11.cloned.1.call-update) | async-done | bytes 4194320 | tf_op jit(solution)/shard_map/all_gather | solution.py:180
  391.9 3.8 fusion.120
  399.6 5.6 fusion.126
  405.2 5.5 fusion.129
  410.6 3.9 fusion.170
  416.5 4.1 fusion.114
  420.7 11.8 %fusion.132 = f32[1,512,2,128]{3,1,2,0:T(8,128)} fusion(bf16[1024,2,128]{2,0,1:T(8,128)(2,1)} %copy-done.35, f32[2,512,1024]{2,1,0:T(8,128)} %fusion.170, f32[2,512,1024]{2,1,0:T(8,128)} %copy-done.2, f32[2,512]{1,0:T(2,128)S(1)} %log_add_fusion), kind=kOutput, calls=%fused_computation.104 | convolution fusion | flops 275777536 | bytes 9441280 | tf_op jit(solution)/shard_map/shqk,skhd->sqhd/dot_general | solution.py:68
  434.6 15.6 %broadcast_multiply_fusion = (f32[1,1024,2,128]{3,1,2,0:T(8,128)}, f32[1,1024,2,128]{3,1,2,0:T(8,128)}, f32[1,1024,2,128]{3,1,2,0:T(8,128)}) fusion(f32[1024,128]{1,0:T(8,128)} %copy-done.10, f32[1,512,2,128]{3,1,2,0:T(8,128)} %fusion.132, f32[1,512,2,128]{3,1,2,0:T(8,128)} %fusion.126, f32[2,512,1024]{2,1,0:T(8,128)} %fusion.170, ...), kind=kOutput, calls=%fused_computation.157 | convolution fusion | flops 276826112 | bytes 22290432 | tf_op jit(solution)/shard_map/shqk,sqhd->skhd/dot_general | solution.py:68
  457.8 2.5 copy.98
  465.1 3.4 fusion.42
  468.6 6.4 convert_bitcast_fusion
  475.0 7.8 fusion.39
  482.8 4.4 fusion.33
  487.2 4.6 fusion.36
  497.4 3.9 fusion.101
  510.4 10.2 %reduce-scatter.11.cloned.1.call-done = bf16[1,128,2048]{2,1,0:T(8,128)(2,1)} async-done(((bf16[1,1024,2048]{2,1,0:T(8,128)(2,1)}), bf16[1,128,2048]{2,1,0:T(8,128)(2,1)}) %reduce-scatter.11.cloned.1.call-update) | async-done | bytes 524304 | tf_op jit(solution)/shard_map/reduce_scatter | solution.py:229
  522.7 3.3 all-to-all-start
  526.1 2.3 constant_dynamic-update-slice_fusion.1
  528.4 2.7 all-to-all-done
  531.7 43.8 %reduce-scatter.7.cloned.1.call-done = bf16[1,128,2048]{2,1,0:T(8,128)(2,1)} async-done(((bf16[1,1024,2048]{2,1,0:T(8,128)(2,1)}), bf16[1,128,2048]{2,1,0:T(8,128)(2,1)}) %reduce-scatter.7.cloned.1.call-update) | async-done | bytes 524304 | tf_op jit(solution)/shard_map/reduce_scatter | solution.py:151
  575.5 3.6 fusion.137
  579.1 285.4 %all-reduce.5.cloned.1.call-done = (bf16[2097664]{0:T(1024)(128)(2,1)}, bf16[2048,688]{0,1:T(8,128)(2,1)}, bf16[2048,688]{0,1:T(8,128)(2,1)}, bf16[688,2048]{1,0:T(8,128)(2,1)}) async-done(((bf16[2097664]{0:T(1024)(128)(2,1)}, bf16[2048,688]{0,1:T(8,128)(2,1)}, bf16[2048,688]{0,1:T(8,128)(2,1)}, bf16[688,2048]{1,0:T(8,128)(2,1)}), (bf16[2097664]{0:T(1024)(128)(2,1)}, bf16[2048,688]{0,1:T(8,128)(2,1)}, ...) | async-done | bytes 12649488 | tf_op jit(solution)/shard_map/psum | solution.py:29
  865.2 5.8 slice_convert_fusion
  871.6 3.2 convert_element_type.278
  874.8 2.7 reshape.908
  877.5 2.9 reshape.907
  880.4 2.9 reshape.906
  883.2 2.9 reshape.905
  886.1 5.2 convert_element_type.280
  891.3 3.2 convert_element_type.282
  (200 shorter events, 75.5 us)
Async XLA Ops:
  7.2 259.7 %copy-start = (bf16[688,2048]{1,0:T(8,128)(2,1)S(1)}, bf16[688,2048]{1,0:T(8,128)(2,1)}, u32[]{:S(2)}) copy-start(bf16[688,2048]{1,0:T(8,128)(2,1)} %param.30) | copy-start | bytes 8454148
  7.2 59.5 %all-gather.5.cloned.1.call-start = ((), (), s32[]{:S(2)}) async-start(), calls=%async_computation.5 | async-start | bytes 4718592 | tf_op jit(solution)/shard_map/all_gather | solution.py:101
  10.7 148.4 %reduce-scatter.5.cloned.1.call-start = ((), (), s32[]{:S(2)}) async-start(), calls=%async_computation.6 | async-start | bytes 4718592 | tf_op jit(solution)/shard_map/reduce_scatter | solution.py:138
  13.0 84.9 %copy-start.4 = (f32[1024,128]{1,0:T(8,128)}, f32[1024,128]{1,0:T(8,128)S(1)}, u32[]{:S(2)}) copy-start(f32[1024,128]{1,0:T(8,128)S(1)} %get-tuple-element.116) | copy-start | bytes 1572868
  92.2 7.0 copy-start.34
  92.7 2.3 copy-start.41
  93.5 2.6 copy-start.29
  94.1 3.3 copy-start.7
  97.4 4.4 copy-start.25
  97.9 5.0 copy-start.51
  100.3 2.6 copy-start.2
  101.8 1.9 copy-start.50
  107.0 52.1 %copy-start.1 = (bf16[1,128,2048]{2,1,0:T(8,128)(2,1)S(1)}, bf16[1,128,2048]{2,1,0:T(8,128)(2,1)}, u32[]{:S(2)}) copy-start(bf16[1,128,2048]{2,1,0:T(8,128)(2,1)} %param.23) | copy-start | bytes 1572868
  107.0 53.4 %copy-start.39 = (f32[2048]{0:T(1024)S(1)}, f32[2048]{0:T(1024)}, u32[]{:S(2)}) copy-start(f32[2048]{0:T(1024)} %param.32) | copy-start | bytes 24580
  107.0 106.9 %all-gather.7.cloned.1.call-start = ((), (), s32[]{:S(2)}) async-start(), calls=%async_computation.7 | async-start | bytes 4718592 | tf_op jit(solution)/shard_map/all_gather | solution.py:144
  162.4 104.4 %all-gather.9.cloned.1.call-start = ((), (), s32[]{:S(2)}) async-start(), calls=%async_computation.9 | async-start | bytes 4718592 | tf_op jit(solution)/shard_map/all_gather | solution.py:156
  163.0 173.0 %reduce-scatter.9.cloned.1.call-start = ((), (), s32[]{:S(2)}) async-start(), calls=%async_computation.10 | async-start | bytes 4718592 | tf_op jit(solution)/shard_map/reduce_scatter | solution.py:170
  213.9 7.9 copy-start.44
  213.9 7.9 copy-start.47
  266.8 8.2 copy-start.48
  275.0 3.6 copy-start.55
  275.0 3.6 copy-start.57
  275.1 3.6 copy-start.49
  284.0 107.9 %all-gather.11.cloned.1.call-start = ((), (), s32[]{:S(2)}) async-start(), calls=%async_computation.11 | async-start | bytes 4718592 | tf_op jit(solution)/shard_map/all_gather | solution.py:180
  340.3 180.2 %reduce-scatter.11.cloned.1.call-start = ((), (), s32[]{:S(2)}) async-start(), calls=%async_computation.12 | async-start | bytes 4718592 | tf_op jit(solution)/shard_map/reduce_scatter | solution.py:229
  391.9 3.9 copy-start.26
  395.7 1.8 copy-start.23
  395.7 2.5 copy-start.8
  450.1 2.0 copy-start.13
  452.2 1.7 copy-start.31
  460.3 2.0 copy-start.27
  468.5 107.0 %reduce-scatter.7.cloned.1.call-start = ((), (), s32[]{:S(2)}) async-start(), calls=%async_computation.8 | async-start | bytes 4718592 | tf_op jit(solution)/shard_map/reduce_scatter | solution.py:151
  475.0 7.8 copy-start.45
  475.0 7.8 copy-start.58
  482.8 4.4 copy-start.56
  487.2 4.6 copy-start.20
  487.2 4.6 copy-start.42
  497.3 5.0 copy-start.18
  497.3 5.0 copy-start.43
  503.7 3.2 copy-start.12
  504.8 3.1 copy-start.46
  504.8 3.1 copy-start.52
  504.8 3.1 copy-start.54
  508.0 12.6 %copy-start.40 = (f32[2048]{0:T(1024)S(1)}, f32[2048]{0:T(1024)}, u32[]{:S(2)}) copy-start(f32[2048]{0:T(1024)} %param.31) | copy-start | bytes 24580
  522.7 8.3 all-to-all-start
  526.0 338.5 %all-reduce.5.cloned.1.call-start = ((), (), s32[]{:S(2)}) async-start(), calls=%async_computation.13 | async-start | bytes 25300992 | tf_op jit(solution)/shard_map/psum | solution.py:29
  865.2 6.4 copy-start.16
  886.1 5.2 copy-start.15
  (21 other events, 25.6 us)
Sparse Core Ops, SparseCore 0:
  10.8 55.8 all-gather.4
  107.1 51.8 reduce-scatter.4
  162.5 51.3 all-gather.6
  215.4 51.3 all-gather.8
  284.1 51.8 reduce-scatter.8
  340.5 51.3 all-gather.10
  468.6 51.9 reduce-scatter.10
  523.6 51.8 reduce-scatter.6
  578.9 285.6 all-reduce.4
where the time goes:
time: 917 us; the launch traced here: 901 us
  waiting for transfers between devices  637 us (69%)
  matrix products  136 us (15%)
  local copies, waits for them, and re-layouts  59.5 us (6%)
  other arithmetic  50 us (5%)
  between operations  14.7 us (2%)
    psum x1, waiting for transfers between devices, packed_total(): subtotal = lax.psum(jnp.concatenate([a.ravel() for a in arrays]), axis)  285 us
    dot_general x33, matrix products, apply_projection(): return jnp.einsum(form, left, right, preferred_element_type=jnp.float32)  136 us
    reduce_scatter x1, waiting for transfers between devices, per_device(): lax.psum_scatter(attention_parts.astype(jnp.bfloat16), 'tensor', scatter_...  52 us
    reduce_scatter x1, waiting for transfers between devices, per_device(): lax.psum_scatter(feedforward_backward_parts.astype(jnp.bfloat16), 'tensor...  52 us
    all_gather x1, waiting for transfers between devices, per_device(): lax.all_gather(normalized_second, 'tensor', axis=1, tiled=True)  50.9 us
    all_gather x1, waiting for transfers between devices, per_device(): lax.all_gather(normalized_first, 'tensor', axis=1, tiled=True)  49.5 us
    all_gather x1, waiting for transfers between devices, per_device(): lax.all_gather(grad_resid.astype(jnp.bfloat16), 'tensor', axis=1, tiled=T...  49.2 us
    reduce_scatter x1, waiting for transfers between devices, per_device(): lax.psum_scatter(feedforward_parts.astype(jnp.bfloat16), 'tensor', scatte...  43.8 us
  transfers between devices with their start and end apart: 10, of which 10 were waited for; matrix products, arithmetic and copies ran while one was open for 8% of the time, Pallas kernels for 0%

commit v1 on v0

v1 whole, which is shorter than its diff:
```python
import functools

import jax
import jax.numpy as jnp
import numpy as np
from jax import lax
from jax.experimental import pallas as pl
from jax.experimental.pallas import tpu as pltpu
from jax.sharding import Mesh, PartitionSpec as P

HEAD_DIM = 128
NORM_EPS = 1e-05
ROPE_BASE = 10000.0
F32, BF16 = jnp.float32, jnp.bfloat16
MESH = pl.DeviceIdType.MESH
ANY = pl.BlockSpec(memory_space=pl.ANY)
VM = pl.BlockSpec(memory_space=pltpu.VMEM)
MIB = 2**20


def tables(length, head_dim):
    half = head_dim // 2
    freqs = np.float32(ROPE_BASE) ** (-(np.float32(2.0) * np.arange(half, dtype=np.float32)) / np.float32(head_dim))
    angles = np.arange(length, dtype=np.float32)[:, None] * freqs[None, :]
    cosine, sine = np.cos(angles), np.sin(angles)
    return np.concatenate([cosine, cosine], 1), np.concatenate([-sine, sine], 1)


class Place:
    def __init__(self):
        self.x = lax.axis_index("x")
        self.zh = lax.axis_index("zh")
        self.zl = lax.axis_index("zl")
        self.c = lax.axis_index("core")
        self.y = lax.axis_index("y")
        self.z = self.zh * 2 + self.zl

    def at(self, dx=0, dy=0, dz=0, core=None):
        out = {}
        if dx:
            out["x"] = lax.rem(self.x + dx + 4, 4)
        if dy:
            out["y"] = lax.rem(self.y + dy + 4, 4)
        if dz:
            z = lax.rem(self.z + dz + 4, 4)
            out["zh"], out["zl"] = z // 2, lax.rem(z, 2)
        if core is not None:
            out["core"] = core
        return out

    def sibling(self):
        return {"core": 1 - self.c}

    def yy(self, d):
        return lax.rem(self.y + d + 4, 4)


def meet(devices):
    barrier = pltpu.get_barrier_semaphore()
    for d in devices:
        pl.semaphore_signal(barrier, inc=1, device_id=d, device_id_type=MESH)
    pl.semaphore_wait(barrier, len(devices))


def remote(src, dst, ss, rs, device):
    return pltpu.make_async_remote_copy(
        src_ref=src, dst_ref=dst, send_sem=ss, recv_sem=rs, device_id=device, device_id_type=MESH
    )


def dot(a, b):
    return jnp.dot(a, b, preferred_element_type=F32)


def dot_nt(a, b):
    return lax.dot_general(a, b, (((1,), (1,)), ((), ())), preferred_element_type=F32)


def dot_tn(a, b):
    return lax.dot_general(a, b, (((0,), (0,)), ((), ())), preferred_element_type=F32)


def normed(values):
    factor = lax.rsqrt(jnp.mean(values * values, axis=-1, keepdims=True) + NORM_EPS)
    return values * factor, factor


class Gather:
    N = 10

    def __init__(self, me, buf, ss, rs, rows):
        h = rows // 2
        c, y = me.c, me.y

        def part(d, lo, n):
            return buf.at[me.yy(d), pl.ds(c * rows + lo, n)]

        up, down, sib = me.at(dy=1), me.at(dy=-1), me.sibling()
        spec = [
            (0, 0, h, up), (0, h, h, up), (0, h, h, down), (0, 0, h, down), (0, 0, rows, sib),
            (-1, 0, h, up), (1, h, h, down), (-1, 0, rows, sib), (1, 0, rows, sib), (2, 0, rows, sib),
        ]
        self.copies = [remote(part(d, lo, n), part(d, lo, n), ss.at[i], rs.at[i], to) for i, (d, lo, n, to) in enumerate(spec)]

    def start(self):
        for i in (0, 2, 1, 3, 4):
            self.copies[i].start()

    def got(self, i):
        self.copies[i].wait_recv()

    def forward_one(self):
        self.got(0)
        self.copies[5].start()
        self.got(2)
        self.copies[6].start()

    def near(self):
        self.got(1)
        self.copies[7].start()
        self.got(3)
        self.copies[8].start()

    def far(self):
        self.got(5)
        self.got(6)
        self.copies[9].start()

    def finish(self):
        for cp in self.copies:
            cp.wait_send()


class Scatter:
    N = 10

    def __init__(self, me, part, own, ra, rb, f1, f2, ss, rs, rows):
        self.me, self.part, self.own, self.rows = me, part, own, rows
        self.ra, self.rb, self.f1, self.f2 = ra, rb, f1, f2
        self.h = rows // 2
        c = me.c
        up, down, sib = me.at(dy=1), me.at(dy=-1), me.sibling()
        h = self.h
        self.order = (2, 1, -1, 0)
        self.sib = {}
        for i, d in enumerate(self.order):
            self.sib[d] = remote(
                part.at[me.yy(d), pl.ds((1 - c) * rows, rows)], own.at[me.yy(d)], ss.at[i], rs.at[i], sib
            )

        def mine(d, lo):
            return part.at[me.yy(d), pl.ds(c * rows + lo, h)]

        self.a2 = remote(mine(2, 0), ra, ss.at[4], rs.at[4], up)
        self.b2 = remote(mine(2, h), rb, ss.at[5], rs.at[5], down)
        self.b1 = remote(mine(1, h), f1.at[pl.ds(h, h)], ss.at[6], rs.at[6], up)
        self.a1 = remote(mine(1, 0), f1.at[pl.ds(0, h)], ss.at[7], rs.at[7], up)
        self.am = remote(mine(-1, 0), f2.at[pl.ds(0, h)], ss.at[8], rs.at[8], down)
        self.bm = remote(mine(-1, h), f2.at[pl.ds(h, h)], ss.at[9], rs.at[9], down)

    def add(self, d, lo, n, other):
        rows = pl.ds(self.me.c * self.rows + lo, n)
        at = self.me.yy(d)
        self.part[at, rows] = (self.part[at, rows].astype(F32) + other.astype(F32)).astype(BF16)

    def ready(self, d):
        self.sib[d].start()

    def stage_two(self):
        self.sib[2].wait_recv()
        self.add(2, 0, self.rows, self.own[self.me.yy(2)])
        self.a2.start()
        self.b2.start()

    def stage_one(self):
        self.sib[1].wait_recv()
        self.add(1, 0, self.rows, self.own[self.me.yy(1)])
        self.b1.start()
        self.sib[-1].wait_recv()
        self.add(-1, 0, self.rows, self.own[self.me.yy(-1)])
        self.am.start()

    def stage_last(self):
        self.a2.wait_recv()
        self.add(1, 0, self.h, self.ra[...])
        self.a1.start()
        self.b2.wait_recv()
        self.add(-1, self.h, self.h, self.rb[...])
        self.bm.start()

    def result(self):
        self.sib[0].wait_recv()
        for cp in (self.b1, self.am, self.a1, self.bm):
            cp.wait_recv()

    def total(self, lo, n):
        me = self.me
        mine = self.part[me.y, pl.ds(me.c * self.rows + lo, n)].astype(F32)
        near = self.f1[pl.ds(lo, n)].astype(F32) + self.f2[pl.ds(lo, n)].astype(F32)
        return mine + self.own[me.y, pl.ds(lo, n)].astype(F32) + near

    def finish(self):
        for cp in (*self.sib.values(), self.a2, self.b2, self.b1, self.a1, self.am, self.bm):
            cp.wait_send()


def scatter_scratch(rows, width):
    return [
        pltpu.VMEM((4, 2 * rows, width), BF16),
        pltpu.VMEM((4, rows, width), BF16),
        pltpu.VMEM((rows // 2, width), BF16),
        pltpu.VMEM((rows // 2, width), BF16),
        pltpu.VMEM((rows, width), BF16),
        pltpu.VMEM((rows, width), BF16),
    ]


def dma(n):
    return pltpu.SemaphoreType.DMA((n,))


def perm(block):
    return (block % 4) * 2 + block // 4


def forward_attention_kernel(
    tok, cot, wq, wk, wv, wo, wg, wu, wd, g1, g2, cosine, sine,
    resid_o, n2_o, tok_o, cot_o, g_o, q_o, k_o, v_o, ho_o, w3_o, wo_o, wg_o, wu_o, wd_o,
    tok_s, g_s, w3_s, wo_s, q_s, k_s, v_s, ho_s, resid_s, n2_s,
    part, own, ra, rb, f1, f2,
    ag_ss, ag_rs, rs_ss, rs_rs, w_ss, w_rs, loc, out_sem,
):
    me = Place()
    c, zl = me.c, me.zl
    rows = tok.shape[0]
    stays = c == zl
    swap = {"zl": 1 - zl, "core": 1 - c}
    others = [me.at(dy=1), me.at(dy=-1), me.sibling()]
    others += [me.at(dz=s, core=k) for s in (1, -1) for k in (0, 1)]
    meet(others)

    z_other = lax.rem(me.z + jnp.where(zl == 0, 3, 1), 4)
    far_z = {"zh": z_other // 2, "zl": lax.rem(z_other, 2), "core": c}

    heads = (wq, wk, wv)

    def halves(i, src, dst_all, axis_rows):
        h = axis_rows // 2
        a = remote(src.at[pl.ds(0, h)], dst_all.at[pl.ds(0, h)], w_ss.at[i], w_rs.at[2 * i], swap)
        b = remote(src.at[pl.ds(h, h)], dst_all.at[pl.ds(h, h)], w_ss.at[i], w_rs.at[2 * i + 1], far_z)
        return a, b

    def w3_part(i):
        return w3_s.at[:, pl.ds(256 * i, 256)]

    moved = [halves(i, w, w3_part(i), w.shape[0]) for i, w in enumerate(heads)]
    moved.append(halves(3, wo, wo_s, wo.shape[0]))
    later = [halves(4, wg, wg_o, wg.shape[0]), halves(5, wu, wu_o, wu.shape[0])]
    ffd = wd.shape[0]
    hd = (ffd // 2) // 16 * 16
    later.append((
        remote(wd.at[pl.ds(0, hd)], wd_o.at[pl.ds(0, hd)], w_ss.at[6], w_rs.at[12], swap),
        remote(wd.at[pl.ds(hd, ffd - hd)], wd_o.at[pl.ds(hd, ffd - hd)], w_ss.at[6], w_rs.at[13], far_z),
    ))
    tok_move = remote(tok, tok_s, w_ss.at[7], w_rs.at[14], swap)
    cot_move = remote(cot, cot_o, w_ss.at[8], w_rs.at[15], swap)
    local = [pltpu.make_async_copy(w, w3_part(i), loc.at[i]) for i, w in enumerate(heads)]
    local.append(pltpu.make_async_copy(wo, wo_s, loc.at[3]))
    local_later = [
        pltpu.make_async_copy(a, b, loc.at[4 + i]) for i, (a, b) in enumerate(((wg, wg_o), (wu, wu_o), (wd, wd_o), (cot, cot_o)))
    ]
    tok_local = pltpu.make_async_copy(tok, tok_s, loc.at[8])

    @pl.when(stays)
    def _():
        tok_local.start()
        for cp in local:
            cp.start()
        for _, b in moved:
            b.start()
        tok_local.wait()

    @pl.when(jnp.logical_not(stays))
    def _():
        tok_move.start()
        tok_move.wait_send()
        for a, _ in moved:
            a.start()
        tok_move.wait_recv()

    out_tok = pltpu.make_async_copy(tok_s, tok_o, out_sem.at[0])
    out_tok.start()
    unit, _ = normed(tok_s[...].astype(F32))
    g_s[me.y, pl.ds(c * rows, rows)] = (unit * g1[...]).astype(BF16)

    gather = Gather(me, g_s, ag_ss, ag_rs, rows)
    gather.start()

    @pl.when(stays)
    def _():
        for cp in local:
            cp.wait()

    @pl.when(jnp.logical_not(stays))
    def _():
        for i in range(8):
            (moved[i // 2][i % 2]).wait_recv()

    def project(d):
        at = me.yy(d)
        out = dot(g_s[at], w3_s[...])
        for half in (0, 1):
            place = pl.ds(pl.multiple_of((at + 4 * half) * rows, rows), rows)
            cs, sn = cosine[place], sine[place]
            for i, ref in enumerate((q_s, k_s, v_s)):
                for head in (0, 1):
                    v = out[half * rows:(half + 1) * rows, i * 256 + head * 128:i * 256 + head * 128 + 128]
                    if i < 2:
                        v = v * cs + pltpu.roll(v, 64, axis=1) * sn
                    ref[head, place] = v.astype(BF16)

    gather.got(4)
    project(0)
    gather.forward_one()
    gather.near()

    @pl.when(stays)
    def _():
        for cp in local_later:
            cp.start()
        for _, b in later:
            b.start()

    @pl.when(jnp.logical_not(stays))
    def _():
        cot_move.start()
        for a, _ in later:
            a.start()

    gather.got(7)
    project(-1)
    gather.got(8)
    project(1)
    gather.far()
    gather.got(9)
    project(2)
    out_g = pltpu.make_async_copy(g_s, g_o, out_sem.at[1])
    out_g.start()
    outs = [out_tok, out_g]
    for i, (a, b) in enumerate(((q_s, q_o), (k_s, k_o), (v_s, v_o), (w3_s, w3_o))):
        cp = pltpu.make_async_copy(a, b, out_sem.at[2 + i])
        cp.start()
        outs.append(cp)

    scale = HEAD_DIM ** (-0.5)
    step = 2 * rows
    for block in range(4):
        stop = (block + 1) * step
        for head in (0, 1):
            s = dot_nt(q_s[head, pl.ds(block * step, step)], k_s[head, pl.ds(0, stop)]) * scale
            places = block * step + lax.broadcasted_iota(jnp.int32, (step, stop), 0)
            s = jnp.where(lax.broadcasted_iota(jnp.int32, (step, stop), 1) <= places, s, -1e30)
            e = jnp.exp(s - jnp.max(s, -1, keepdims=True))
            p = (e / jnp.sum(e, -1, keepdims=True)).astype(BF16)
            o = dot(p, v_s[head, pl.ds(0, stop)]).astype(BF16)
            for half in (0, 1):
                ho_s[pl.ds(perm(2 * block + half) * rows, rows), pl.ds(head * 128, 128)] = o[half * rows:(half + 1) * rows]
    for i, (a, b) in enumerate(((ho_s, ho_o), (wo_s, wo_o))):
        cp = pltpu.make_async_copy(a, b, out_sem.at[6 + i])
        cp.start()
        outs.append(cp)

    scatter = Scatter(me, part, own, ra, rb, f1, f2, rs_ss, rs_rs, rows)

    def out_project(d):
        at = me.yy(d)
        part[at] = dot(ho_s[pl.ds(pl.multiple_of(at * 2 * rows, 2 * rows), 2 * rows)], wo_s[...]).astype(BF16)
        scatter.ready(d)

    out_project(2)
    out_project(1)
    out_project(-1)
    scatter.stage_two()
    out_project(0)
    scatter.stage_one()
    scatter.stage_last()
    scatter.result()
    resid = tok_s[...].astype(F32) + scatter.total(0, rows)
    resid_s[...] = resid
    unit, _ = normed(resid)
    n2_s[...] = (unit * g2[...]).astype(BF16)
    for i, (a, b) in enumerate(((resid_s, resid_o), (n2_s, n2_o))):
        cp = pltpu.make_async_copy(a, b, out_sem.at[8 + i])
        cp.start()
        outs.append(cp)

    gather.finish()
    scatter.finish()
    for cp in outs:
        cp.wait()

    @pl.when(stays)
    def _():
        for cp in local_later:
            cp.wait()
        for _, b in moved + later:
            b.wait_send()

    @pl.when(jnp.logical_not(stays))
    def _():
        cot_move.wait()
        for a, b in later:
            a.wait()
            b.wait_recv()
        for a, _ in moved:
            a.wait_send()


def forward_attention(args):
    tok, cot, wq, wk, wv, wo, wg, wu, wd, g1, g2, cosine, sine = args
    rows, width = tok.shape
    ff = wg.shape[1]
    length = 8 * rows
    sds = jax.ShapeDtypeStruct
    outs = [
        sds((rows, width), F32), sds((rows, width), BF16), sds((rows, width), BF16), sds((rows, width), BF16),
        sds((4, 2 * rows, width), BF16),
        sds((2, length, 128), BF16), sds((2, length, 128), BF16), sds((2, length, 128), BF16),
        sds((length, 256), BF16), sds((width, 768), BF16), sds((256, width), BF16),
        sds((width, ff), BF16), sds((width, ff), BF16), sds((ff, width), BF16),
    ]
    scratch = [
        pltpu.VMEM((rows, width), BF16), pltpu.VMEM((4, 2 * rows, width), BF16),
        pltpu.VMEM((width, 768), BF16), pltpu.VMEM((256, width), BF16),
        *[pltpu.VMEM((2, length, 128), BF16)] * 3, pltpu.VMEM((length, 256), BF16),
        pltpu.VMEM((rows, width), F32), pltpu.VMEM((rows, width), BF16),
        *scatter_scratch(rows, width),
        dma(10), dma(10), dma(10), dma(10), dma(9), dma(16), dma(9), dma(10),
    ]
    return pl.pallas_call(
        forward_attention_kernel,
        name="forward_attention",
        out_shape=outs,
        in_specs=[ANY] * 9 + [VM] * 4,
        out_specs=[ANY] * len(outs),
        scratch_shapes=scratch,
        compiler_params=pltpu.CompilerParams(collective_id=0, has_side_effects=True, vmem_limit_bytes=60 * MIB),
    )(*args)


def norm_back(grads, unit, factor):
    return factor * (grads - unit * jnp.mean(grads * unit, axis=-1, keepdims=True))


TP = ("core", "y")
DP = ("x", "zh", "zl")
SWAP = [(0, 0), (1, 2), (2, 1), (3, 3)]


def natural(g):
    rows = g.shape[1] // 2
    return g.reshape(4, 2, rows, -1).transpose(1, 0, 2, 3).reshape(8 * rows, -1)


def per_device(tokens, wq, wk, wv, wo, wg, wu, wd, attn_gain, mlp_gain, cotangent):
    tokens, cotangent = tokens[0], cotangent[0]
    rows = tokens.shape[0]
    length = 8 * rows
    cosine, sine = (jnp.asarray(t) for t in tables(length, HEAD_DIM))
    (resid, n2, tok, cot, g1, q, k, v, ho, w3, wo, wg, wu, wd) = forward_attention(
        (tokens, cotangent, wq, wk, wv, wo, wg, wu, wd, attn_gain[None], mlp_gain[None], cosine, sine)
    )
    inputs = tok.astype(F32)
    grad_out = cot.astype(F32)
    one = natural(g1)
    ho = natural(ho.reshape(4, 2 * rows, 256))
    unit_one, factor_one = normed(inputs)
    unit_two, factor_two = normed(resid)

    def gathered(x):
        return lax.all_gather(x, TP, axis=0, tiled=True)

    def scattered(x):
        return lax.psum_scatter(x.astype(BF16), TP, scatter_dimension=0, tiled=True).astype(F32)

    two = gathered(n2)
    gate, up = dot(two, wg), dot(two, wu)
    sigma = jax.nn.sigmoid(gate)
    swish = gate * sigma
    hidden = (swish * up).astype(BF16)
    activations = (resid + scattered(dot(hidden, wd))).astype(BF16)
    gm = gathered(cot)
    d_wd = dot_tn(hidden, gm)
    gh = dot_nt(gm, wd)
    d_gate = (gh * up * sigma * (1.0 + gate * (1.0 - sigma))).astype(BF16)
    d_up = (gh * swish).astype(BF16)
    d_wg, d_wu = dot_tn(two, d_gate), dot_tn(two, d_up)
    gn2 = scattered(dot_nt(d_gate, wg) + dot_nt(d_up, wu))
    gain_two = jnp.sum(gn2 * unit_two, axis=0)
    grad_resid = grad_out + norm_back(gn2 * mlp_gain, unit_two, factor_two)
    ga = gathered(grad_resid.astype(BF16))
    d_wo = dot_tn(ho, ga)
    gheads = dot_nt(ga, wo).astype(BF16).reshape(length, 2, 128).transpose(1, 0, 2)
    scale = HEAD_DIM ** (-0.5)
    seen = jnp.tril(jnp.ones((length, length), bool))
    s = jnp.where(seen, jnp.einsum("hqd,hkd->hqk", q, k, preferred_element_type=F32) * scale, -1e30)
    p = jax.nn.softmax(s, -1)
    gv = jnp.einsum("hqk,hqd->hkd", p.astype(BF16), gheads, preferred_element_type=F32).astype(BF16)
    gp = jnp.einsum("hqd,hkd->hqk", gheads, v, preferred_element_type=F32)
    gs = (p * (gp - jnp.sum(p * gp, -1, keepdims=True)) * scale).astype(BF16)
    gq = jnp.einsum("hqk,hkd->hqd", gs, k, preferred_element_type=F32)
    gk = jnp.einsum("hqk,hqd->hkd", gs, q, preferred_element_type=F32)

    def unrotate(g):
        return (g * cosine - jnp.roll(g, 64, -1) * sine).astype(BF16)

    def flat(g):
        return g.transpose(1, 0, 2).reshape(length, 256)

    g3 = jnp.concatenate([flat(unrotate(gq)), flat(unrotate(gk)), flat(gv)], 1)
    d_w3 = dot_tn(one, g3)
    gn1 = scattered(dot_nt(g3, w3))
    gain_one = jnp.sum(gn1 * unit_one, axis=0)
    input_grad = grad_resid + norm_back(gn1 * attn_gain, unit_one, factor_one)
    gains = lax.psum(jnp.stack([gain_one, gain_two]), ("x", "zh", "zl", "core", "y"))
    place = lax.axis_index("zl") * 4 + lax.axis_index("y")
    gains = lax.dynamic_slice_in_dim(gains, place * 256, 256, 1)
    zl = lax.axis_index("zl")

    def total(x):
        x = lax.psum(x.astype(BF16), DP)
        both = lax.all_gather(x, "core", axis=0)
        return lax.dynamic_index_in_dim(both, zl, 0, keepdims=False).astype(F32)

    d_w3 = total(d_w3)

    def back(x):
        return lax.ppermute(x, ("core", "zl"), SWAP)[None]

    return (
        back(activations), back(input_grad), d_w3[:, :256], d_w3[:, 256:512], d_w3[:, 512:], total(d_wo),
        total(d_wg), total(d_wu), total(d_wd), gains[0], gains[1],
    )


def solution(mesh):
    split = Mesh(mesh.devices.reshape(4, 2, 2, 2, 4), ("x", "zh", "core", "zl", "y"))
    dp, tensor = ("x", "zh", "core"), ("zl", "y")
    cols, rows, seqs = P(None, tensor), P(tensor, None), P(dp, tensor, None)
    return jax.shard_map(
        per_device,
        mesh=split,
        in_specs=(seqs, cols, cols, cols, rows, cols, cols, rows, P(), P(), seqs),
        out_specs=(seqs, seqs, cols, cols, cols, rows, cols, cols, rows, P(tensor), P(tensor)),
        check_vma=False,
    )
```

time: 917 us -> 965 us (1.052)
  Pallas kernels: 0 us -> 96.2 us
  blocking collectives: 0 us -> 72.7 us
  waiting for transfers between devices: 637 us -> 595 us
  local copies, waits for them, and re-layouts: 59.5 us -> 27.5 us
  matrix products: 136 us -> 113 us
  other arithmetic: 50 us -> 30.6 us
    psum x1, waiting for transfers between devices: 285 us -> 164 us  [total(): x = lax.psum(x.astype(BF16), DP)]
    pallas_call x0 -> x1, Pallas kernels: none -> 96.2 us  [forward_attention(): pl.pallas_call(forward_attention_kernel, name='forward_attention', out_sh...]
    all_gather x4 -> x8, waiting for transfers between devices: 190 us -> 271 us  [the longest x3 270 us: gathered(): return lax.all_gather(x, TP, axis=0, tiled=True)]
    psum x0 -> x1, blocking collectives: none -> 72.7 us  [per_device(): lax.psum(jnp.stack([gain_one, gain_two]), ('x', 'zh', 'zl', 'core', 'y'))]
    dot_general x33 -> x17, matrix products: 136 us -> 106 us  [the longest x5 29.3 us: dot_nt(): lax.dot_general(a, b, (((1,), (1,)), ((), ())), preferred_element_type=F32)]
    convert_element_type x6 -> x0, local copies, waits for them, and re-layouts: 15.4 us -> none  [the longest x4 11.3 us: per_device(): part.astype(jnp.float32)]
    unnamed x131 -> x72, local copies, waits for them, and re-layouts: 27.9 us -> 16.8 us
    convert_element_type x12 -> x7, other arithmetic: 29.5 us -> 24.1 us  [the longest x5 21.3 us: total(): return lax.dynamic_index_in_dim(both, zl, 0, keepdims=False).astype(F32)]
  transfers between devices with their start and end apart: 10 -> 14, of which waited for: 10 -> 8; matrix products, arithmetic and copies ran while one was open for 8% -> 8% of each run, Pallas kernels for 0% -> 0%
where the time goes in v1:
time: 965 us; the launch traced here: 957 us
  waiting for transfers between devices  595 us (62%)
  matrix products  113 us (12%)
  Pallas kernels  96.2 us (10%)
  blocking collectives  72.7 us (8%)
  other arithmetic  30.6 us (3%)
  local copies, waits for them, and re-layouts  27.5 us (3%)
  between operations  15 us (2%)
    all_gather x3, waiting for transfers between devices, gathered(): return lax.all_gather(x, TP, axis=0, tiled=True)  270 us
    psum x1, waiting for transfers between devices, total(): x = lax.psum(x.astype(BF16), DP)  164 us
    reduce_scatter x3, waiting for transfers between devices, scattered(): lax.psum_scatter(x.astype(BF16), TP, scatter_dimension=0, tiled=True)  156 us
    pallas_call x1, Pallas kernels, forward_attention(): pl.pallas_call(forward_attention_kernel, name='forward_attention', out_sh...  96.2 us
    psum x1, blocking collectives, per_device(): lax.psum(jnp.stack([gain_one, gain_two]), ('x', 'zh', 'zl', 'core', 'y'))  72.7 us
    dot_general x5, matrix products, dot_nt(): lax.dot_general(a, b, (((1,), (1,)), ((), ())), preferred_element_type=F32)  29.3 us
    dot_general x5, matrix products, dot_tn(): lax.dot_general(a, b, (((0,), (0,)), ((), ())), preferred_element_type=F32)  23.9 us
    convert_element_type x5, other arithmetic, total(): return lax.dynamic_index_in_dim(both, zl, 0, keepdims=False).astype(F32)  21.3 us
  transfers between devices with their start and end apart: 14, of which 8 were waited for; matrix products, arithmetic and copies ran while one was open for 8% of the time, Pallas kernels for 0%

profile of v1, /device:TPU:1, one launch (start us, length us, event | category | flops | bytes accessed | tf_op | source)
XLA Modules:
  0.0 956.5 jit_solution(3791572300404925913)
XLA Ops:
  7.2 4.6 copy.46.wg
  11.8 4.6 copy.47.wu
  16.4 96.2 %forward_attention.1 = (f32[128,2048]{1,0:T(8,128)}, bf16[128,2048]{1,0:T(8,128)(2,1)}, bf16[128,2048]{1,0:T(8,128)(2,1)}, bf16[128,2048]{1,0:T(8,128)(2,1)}, bf...) custom-call(bf16[128,2048]{1,0:T(8,128)(2,1)} %bitcast.91, ...), custom_call_target="tpu_custom_call" | custom-call | tf_op jit(solution)/shard_map/forward_attention/pallas_call | solution.py:440
  114.0 246.4 %all-gather.9.cloned.1.call-done = bf16[1024,2048]{1,0:T(8,128)(2,1)} async-done(((bf16[128,2048]{1,0:T(8,128)(2,1)}), bf16[1024,2048]{1,0:T(8,128)(2,1)}) %all-gather.9.cloned.1.call-update) | async-done | bytes 4194320 | tf_op jit(solution)/shard_map/all_gather | solution.py:481
  360.4 8.0 fusion.61
  368.4 4.8 fusion.60
  373.2 21.0 %all-gather.11.cloned.1.call-done = bf16[1024,2048]{1,0:T(8,128)(2,1)} async-done(((bf16[128,2048]{1,0:T(8,128)(2,1)}), bf16[1024,2048]{1,0:T(8,128)(2,1)}) %all-gather.11.cloned.1.call-update) | async-done | bytes 4194320 | tf_op jit(solution)/shard_map/all_gather | solution.py:481
  394.2 10.0 %multiply_convert_fusion.1 = (bf16[1024,688]{0,1:T(8,128)(2,1)S(1)}, bf16[1024,688]{0,1:T(8,128)(2,1)S(1)}, bf16[1024,688]{0,1:T(8,128)(2,1)}) fusion(f32[1024,688]{0,1:T(8,128)} %fusion.60, f32[1024,688]{0,1:T(8,128)} %fusion.61, bf16[1024,2048]{1,0:T(8,128)(2,1)} %all-gather.11.cloned.1.call-done, bf16[688,2048]{1,0:T(8,128)(2,1)} %get-tuple-element.29), kind=kOutput, calls=%fused_computation.32 | convolution fusion | flops 2896248832 | bytes 16875520 | tf_op jit(solution)/shard_map/dot_general | solution.py:76
  404.2 3.7 fusion.62
  407.9 5.1 add_convert_fusion
  413.1 1.1 copy-done
  414.4 50.6 %reduce-scatter.6.cloned.1.call-done = bf16[128,2048]{1,0:T(8,128)(2,1)} async-done(((bf16[1024,2048]{1,0:T(8,128)(2,1)}), bf16[128,2048]{1,0:T(8,128)(2,1)}) %reduce-scatter.6.cloned.1.call-update) | async-done | bytes 524304 | tf_op jit(solution)/shard_map/reduce_scatter | solution.py:484
  465.0 1.4 fusion.36
  466.4 2.2 fusion.54
  469.5 4.8 copy.56
  474.7 7.6 fusion.59
  482.3 7.4 fusion.20
  489.7 4.7 fusion.19
  494.4 4.4 fusion.18
  498.8 2.1 all-gather.13.cloned.1.call-done
  501.0 3.6 convolution_convert_fusion.7
  504.6 4.5 fusion.63
  509.1 2.3 fusion.25
  511.5 12.4 %fusion.15 = f32[2,1024,128]{1,2,0:T(8,128)S(1)} fusion(bf16[2,1024,128]{2,1,0:T(8,128)(2,1)} %get-tuple-element.33, f32[2,1024,1024]{1,2,0:T(8,128)} %fusion.63, f32[2,1024,1024]{1,2,0:T(8,128)} %get-tuple-element.65, f32[2,1024]{1,0:T(2,128)S(1)} %get-tuple-element.64), kind=kOutput, calls=%fused_computation.19 | convolution fusion | flops 551554048 | bytes 18358272 | tf_op jit(solution)/shard_map/hqk,hkd->hqd/dot_general | solution.py:511
  523.9 13.4 %fusion.12 = f32[2,1024,128]{1,2,0:T(8,128)} fusion(bf16[2,1024,128]{2,1,0:T(8,128)(2,1)S(1)} %copy-done.24, f32[2,1024,1024]{1,2,0:T(8,128)} %fusion.63, f32[2,1024,1024]{1,2,0:T(8,128)} %get-tuple-element.65, f32[2,1024]{1,0:T(2,128)S(1)} %get-tuple-element.64), kind=kOutput, calls=%fused_computation.18 | convolution fusion | flops 551554048 | bytes 18358272 | tf_op jit(solution)/shard_map/hqk,hqd->hkd/dot_general | solution.py:512
  537.3 1.5 fusion.56
  539.9 1.5 copy-done.4
  541.4 5.1 fusion.17
  546.6 2.2 fusion.22
  550.0 6.9 convolution_convert_fusion.1
  557.0 1.7 copy-done.30
  558.7 6.8 convolution_convert_fusion
  565.6 164.3 %all-reduce.3.cloned.1.call-done = (bf16[1,2048,768]{2,1,0:T(8,128)(2,1)}, bf16[1,256,2048]{2,1,0:T(8,128)(2,1)}, bf16[1,2048,688]{1,2,0:T(8,128)(2,1)}, bf16[1,...) async-done(((bf16[1,2048,768]{2,1,0:T(8,128)(2,1)}, bf16[1,256,2048]{2,1,0:T(8,128)(2,1)}, bf16[1,2048,688]{1,2,0:T(8,128)(2,1)}, bf16[1,2048,688]{1,2,0:T(8,128)(2,1)}, ...) | async-done | bytes 12648464 | tf_op jit(solution)/shard_map/psum | solution.py:531
  732.8 52.0 %reduce-scatter.8.cloned.1.call-done = bf16[128,2048]{1,0:T(8,128)(2,1)} async-done(((bf16[1024,2048]{1,0:T(8,128)(2,1)}), bf16[128,2048]{1,0:T(8,128)(2,1)}) %reduce-scatter.8.cloned.1.call-update) | async-done | bytes 524304 | tf_op jit(solution)/shard_map/reduce_scatter | solution.py:484
  784.8 1.5 fusion.39
  786.3 53.5 %reduce-scatter.4.cloned.1.call-done = bf16[128,2048]{1,0:T(8,128)(2,1)} async-done(((bf16[1024,2048]{1,0:T(8,128)(2,1)}), bf16[128,2048]{1,0:T(8,128)(2,1)}) %reduce-scatter.4.cloned.1.call-update) | async-done | bytes 524304 | tf_op jit(solution)/shard_map/reduce_scatter | solution.py:484
  839.8 2.9 fusion.32
  842.7 3.4 collective-permute-start.1
  846.1 2.1 collective-permute-start
  848.3 72.7 %psum.47 = f32[2,2048]{1,0:T(2,128)S(1)} all-reduce(f32[2,2048]{1,0:T(2,128)S(1)} %pad_maximum_fusion.3), channel_id=1, replica_groups=mesh['x'=4,'zh'=2,'core'=2,'zl'=2,'y'=4] {'x','zh','zl','core','y'}, use_global_device_ids=true, to_apply=%region_17.18 | all-reduce | flops 4096 | bytes 32768 | tf_op jit(solution)/shard_map/psum | solution.py:525
  921.7 2.8 bitcast_convert_fusion.4
  924.5 5.0 bitcast_convert_fusion.3
  929.5 5.6 bitcast_convert_fusion.2
  935.1 5.5 bitcast_convert_fusion.1
  940.5 1.7 all-gather.15.cloned.1.call-done
  942.2 2.4 bitcast_convert_fusion
  944.6 2.8 fusion.55
  948.2 1.0 copy.72
  (108 shorter events, 9.5 us)
Async XLA Ops:
  7.2 353.2 %all-gather.9.cloned.1.call-start = ((), (), s32[]{:S(2)}) async-start(), calls=%async_computation.3 | async-start | bytes 4718592 | tf_op jit(solution)/shard_map/all_gather | solution.py:481
  112.6 281.6 %all-gather.11.cloned.1.call-start = ((), (), s32[]{:S(2)}) async-start(), calls=%async_computation.5 | async-start | bytes 4718592 | tf_op jit(solution)/shard_map/all_gather | solution.py:481
  113.4 351.6 %reduce-scatter.6.cloned.1.call-start = ((), (), s32[]{:S(2)}) async-start(), calls=%async_computation.6 | async-start | bytes 4718592 | tf_op jit(solution)/shard_map/reduce_scatter | solution.py:484
  360.4 8.0 copy-start.15
  360.4 8.0 copy-start.20
  394.2 10.0 %copy-start.21 = (bf16[2048,688]{1,0:T(8,128)(2,1)S(1)}, bf16[2048,688]{1,0:T(8,128)(2,1)}, u32[]{:S(2)}) copy-start(bf16[2048,688]{1,0:T(8,128)(2,1)} %get-tuple-element.27) | copy-start | bytes 8454148
  404.2 3.7 copy-start.27
  404.2 3.8 copy-start.31
  404.2 3.8 copy-start.19
  413.0 1.2 copy-start
  413.0 51.9 %copy-start.13 = (f32[2048]{0:T(1024)S(1)}, f32[2048]{0:T(1024)}, u32[]{:S(2)}) copy-start(f32[2048]{0:T(1024)} %param.22) | copy-start | bytes 24580
  413.0 53.4 %copy-start.1 = (bf16[128,2048]{1,0:T(8,128)(2,1)S(1)}, bf16[128,2048]{1,0:T(8,128)(2,1)}, u32[]{:S(2)}) copy-start(bf16[128,2048]{1,0:T(8,128)(2,1)} %get-tuple-element.30) | copy-start | bytes 1572868
  413.0 55.6 %copy-start.11 = (bf16[1024,256]{1,0:T(8,128)(2,1)S(1)}, bf16[1024,256]{1,0:T(8,128)(2,1)}, u32[]{:S(2)}) copy-start(bf16[1024,256]{1,0:T(8,128)(2,1)} %get-tuple-element.38) | copy-start | bytes 1572868
  413.1 87.9 %all-gather.13.cloned.1.call-start = ((), (), s32[]{:S(2)}) async-start(), calls=%async_computation.7 | async-start | bytes 4718592 | tf_op jit(solution)/shard_map/all_gather | solution.py:481
  468.6 261.2 %all-reduce.3.cloned.1.call-start = ((), (), s32[]{:S(2)}) async-start(), calls=%async_computation.14 | async-start | bytes 25296896 | tf_op jit(solution)/shard_map/psum | solution.py:531
  469.5 5.2 copy-start.23
  482.3 7.4 copy-start.16
  482.3 7.4 copy-start.28
  489.7 4.7 copy-start.17
  489.7 4.7 copy-start.29
  494.4 6.6 copy-start.22
  498.8 5.8 copy-start.8
  501.0 8.1 slice-start
  504.6 4.5 slice-start.1
  511.5 12.5 %copy-start.24 = (bf16[2,1024,128]{2,1,0:T(8,128)(2,1)S(1)}, bf16[2,1024,128]{2,1,0:T(8,128)(2,1)}, u32[]{:S(2)}) copy-start(bf16[2,1024,128]{2,1,0:T(8,128)(2,1)} %get-tuple-element.32) | copy-start | bytes 1572868
  537.3 1.6 copy-start.5
  537.3 1.7 copy-start.6
  537.3 1.8 copy-start.7
  538.9 2.4 copy-start.4
  538.9 2.5 copy-start.25
  539.8 6.7 copy-start.9
  541.4 5.2 copy-start.12
  541.4 5.2 copy-start.18
  548.8 1.0 copy-start.10
  548.8 1.2 copy-start.26
  548.8 235.9 %reduce-scatter.8.cloned.1.call-start = ((), (), s32[]{:S(2)}) async-start(), calls=%async_computation.8 | async-start | bytes 4718592 | tf_op jit(solution)/shard_map/reduce_scatter | solution.py:484
  557.0 1.8 copy-start.30
  557.0 282.8 %reduce-scatter.4.cloned.1.call-start = ((), (), s32[]{:S(2)}) async-start(), calls=%async_computation.4 | async-start | bytes 4718592 | tf_op jit(solution)/shard_map/reduce_scatter | solution.py:484
  565.6 356.1 %all-gather.17.cloned.1.call-start = ((), (), s32[]{:S(2)}) async-start(), calls=%async_computation.10 | async-start | bytes 3145728 | tf_op jit(solution)/shard_map/all_gather | solution.py:532
  729.9 194.5 %all-gather.19.cloned.1.call-start = ((), (), s32[]{:S(2)}) async-start(), calls=%async_computation.11 | async-start | bytes 8454144 | tf_op jit(solution)/shard_map/all_gather | solution.py:532
  730.6 198.9 %all-gather.21.cloned.1.call-start = ((), (), s32[]{:S(2)}) async-start(), calls=%async_computation.12 | async-start | bytes 8454144 | tf_op jit(solution)/shard_map/all_gather | solution.py:532
  730.7 1.9 copy-start.2
  730.7 54.1 %copy-start.14 = (f32[2048]{0:T(1024)S(1)}, f32[2048]{0:T(1024)}, u32[]{:S(2)}) copy-start(f32[2048]{0:T(1024)} %param.21) | copy-start | bytes 24580
  731.2 108.6 %copy-start.3 = (bf16[128,2048]{1,0:T(8,128)(2,1)S(1)}, bf16[128,2048]{1,0:T(8,128)(2,1)}, u32[]{:S(2)}) copy-start(bf16[128,2048]{1,0:T(8,128)(2,1)} %reduce-scatter.6.cloned.1.call-done) | copy-start | bytes 1572868
  731.2 203.8 %all-gather.23.cloned.1.call-start = ((), (), s32[]{:S(2)}) async-start(), calls=%async_computation.13 | async-start | bytes 8454144 | tf_op jit(solution)/shard_map/all_gather | solution.py:532
  732.0 210.2 %all-gather.15.cloned.1.call-start = ((), (), s32[]{:S(2)}) async-start(), calls=%async_computation.9 | async-start | bytes 9437184 | tf_op jit(solution)/shard_map/all_gather | solution.py:532
  842.7 78.9 %collective-permute-start.1 = (f32[128,2048]{1,0:T(8,128)}, f32[128,2048]{1,0:T(8,128)S(1)}, u32[]{:S(2)}, u32[]{:S(2)}) collective-permute-start(f32[128,2048]{1,0:T(8,128)} %get-tuple-element.54), channel_id=1, source_target_pairs={{0,0},{4,8},{8,4},{12,12},{1,1},{5,9},{9,5},{13,13},{2,2},{6,10},{... | collective-permute-start | bytes 3145736 | tf_op jit(solution)/shard_map/ppermute | solution.py:538
  846.1 75.5 %collective-permute-start = (bf16[128,2048]{1,0:T(8,128)(2,1)S(1)}, bf16[128,2048]{1,0:T(8,128)(2,1)S(1)}, u32[]{:S(2)}, u32[]{:S(2)}) collective-permute-start(bf16[128,2048]{1,0:T(8,128)(2,1)S(1)} %get-tuple-element.55), channel_id=1, source_target_pairs={{0,0},{4,8},{8,4},{12,12},{1,1},{5,9},{9,5},{13,13},{2,2},{6,10},{... | collective-permute-start | bytes 1572872 | tf_op jit(solution)/shard_map/ppermute | solution.py:538
Sparse Core Ops, SparseCore 0:
  112.8 247.5 all-gather.8
  362.1 32.0 all-gather.10
  413.2 51.7 reduce-scatter.5
  468.8 32.1 all-gather.12
  549.0 180.8 all-reduce.2
  732.8 51.8 reduce-scatter.7
  787.9 51.8 reduce-scatter.3
  841.6 13.3 all-gather.16
  856.7 19.8 all-gather.18
  878.3 19.7 all-gather.20
  899.9 19.8 all-gather.22
  921.4 20.7 all-gather.14
